TPU v7x, 256 devices: a whole 4x4x8 slice. The times are simulated.
256 devices in a mesh: req: 64 (over y, z_hi, x, core), head: 4 (over z_lo).
Axes of the slice: x: 4, y: 4, z: 8 (z_hi: 2, z_lo: 4; z = z_hi * 4 + z_lo), core: 2. Of those that a mesh axis runs over, the one named last changes fastest.
Arguments:
- kv_cache: bfloat16 [512, 4, 512, 192], P('req', 'head'), may hold values from -6 to 6
- first_fresh: bfloat16 [512, 4, 192], P('req', 'head'), may hold values from -6 to 6
- second_fresh: bfloat16 [512, 4, 192], P('req', 'head'), may hold values from -6 to 6
- first_query: bfloat16 [512, 4, 1024], P('req', 'head'), may hold values from -272 to 272
- second_query: bfloat16 [512, 4, 1024], P('req', 'head'), may hold values from -272 to 272
- key_basis: bfloat16 [4, 64, 128], P('head'), may hold values from -0.75 to 0.75
- out_weight: bfloat16 [4096, 4096], P('head'), may hold values from -1.5 to 1.5
- lengths: int32 [64, 8], replicated, may hold values from 128 to 384, as said below
- leave_slot: int32 [64, 4], replicated, may hold values from 0 to 7, as said below
- arrive_row: int32 [64, 4], replicated, may hold values from 0 to 511, as said below
Outputs:
- first_out: bfloat16 [512, 4096], P('req', 'head')
- second_out: bfloat16 [512, 4096], P('req', 'head')
- final_cache: bfloat16 [512, 4, 512, 192], P('req', 'head')
Inputs may be any that keep to these rules, and one draw needn't show every extreme that they name: `lengths`: A multiple of 128; in every group some row has exactly 384 tokens. `leave_slot`: the 4 slots of a group are distinct. `arrive_row`: the targets are exactly the rows that are left, each once; no group sends two rows to the same group.
All inputs are finite; a program needn't handle non-finite values.
Results may differ from a plain program's by a relative error of at most 0.015.
The roundings to bfloat16 on the way count: a program that leaves them out, or rounds other values in their place, can miss the bound.
Values may be sent and summed in bfloat16 or wider, within the bound.
A program may use at most 128 MiB of HBM per device.

v0:
```python
import math

import jax
import jax.numpy as jnp
from jax import lax
from jax.sharding import PartitionSpec as P


def insert_token(cache_rows, fresh_rows, position):
    slots = jnp.arange(cache_rows.shape[1], dtype=jnp.int32)
    hit_mask = slots[None, :, None] == position[:, None, None]
    return jnp.where(hit_mask, fresh_rows[:, None, :], cache_rows)


def attend_rows(cache_rows, position, query_rows, basis, out_weight):
    row_count = cache_rows.shape[0]
    rank_width = basis.shape[0]
    head_size = basis.shape[1]
    query_heads = query_rows.shape[1] // head_size
    factors = cache_rows[:, :, :rank_width]
    value_part = cache_rows[:, :, rank_width:]
    queries = query_rows.reshape(row_count, query_heads, head_size)
    reduced = jnp.einsum("rqe,ke->rqk", queries, basis, preferred_element_type=jnp.float32).astype(
        jnp.bfloat16
    )
    scores = jnp.einsum("rtk,rqk->rqt", factors, reduced, preferred_element_type=jnp.float32) * (
        1.0 / math.sqrt(head_size)
    )
    live_mask = (
        jnp.arange(cache_rows.shape[1], dtype=jnp.int32)[None, None, :] <= position[:, None, None]
    )
    scores = jnp.where(live_mask, scores, -1e30)
    highest = jnp.max(scores, axis=-1, keepdims=True)
    raw_weights = jnp.exp(scores - highest)
    weights = (raw_weights / jnp.sum(raw_weights, axis=-1, keepdims=True)).astype(jnp.bfloat16)
    attended = jnp.einsum(
        "rqt,rte->rqe", weights, value_part, preferred_element_type=jnp.float32
    ).astype(jnp.bfloat16)
    attended = attended.reshape(row_count, query_heads * head_size)
    partial_value = jnp.dot(attended, out_weight, preferred_element_type=jnp.float32)
    return lax.psum_scatter(
        partial_value.astype(jnp.bfloat16), "head", scatter_dimension=1, tiled=True
    )


def shards(
    kv_cache,
    first_fresh,
    second_fresh,
    first_query,
    second_query,
    key_basis,
    out_weight,
    lengths,
    leave_slot,
    arrive_row,
):
    my_group = lax.axis_index("req")
    group_count = lax.axis_size("req")
    row_count = kv_cache.shape[0]
    move_count = leave_slot.shape[1]
    basis = key_basis[0]
    own_len = lengths[my_group]
    first_cache = insert_token(kv_cache[:, 0], first_fresh[:, 0], own_len)
    first_out = attend_rows(first_cache, own_len, first_query[:, 0], basis, out_weight)
    flat_len = lengths.reshape(-1)
    sources = (jnp.arange(group_count, dtype=jnp.int32)[:, None] * row_count + leave_slot).reshape(
        -1
    )
    targets = arrive_row.reshape(-1)
    moved_len = (
        flat_len.at[targets].set(flat_len[sources]).reshape(group_count, row_count)[my_group]
    )
    match_table = targets[None, :] == sources[:, None]
    flat_ids = jnp.arange(group_count * move_count, dtype=jnp.int32)
    anchor = jnp.sum(jnp.where(match_table, flat_ids[None, :], 0), axis=1)
    own_leave = leave_slot[my_group]
    outgoing = first_cache[own_leave]
    dest_group = arrive_row[my_group] // row_count
    dest_hit = jnp.arange(group_count, dtype=jnp.int32)[:, None] == dest_group[None, :]
    chosen = jnp.sum(
        jnp.where(dest_hit, jnp.arange(move_count, dtype=jnp.int32)[None, :], 0), axis=1
    )
    packed = outgoing[chosen]
    received = lax.all_to_all(packed, "req", split_axis=0, concat_axis=0, tiled=True)
    sender_group = anchor.reshape(group_count, move_count)[my_group] // move_count
    arrived = received[sender_group]
    slot_hit = jnp.arange(row_count, dtype=jnp.int32)[:, None] == own_leave[None, :]
    which_move = jnp.sum(
        jnp.where(slot_hit, jnp.arange(move_count, dtype=jnp.int32)[None, :], 0), axis=1
    )
    present = jnp.any(slot_hit, axis=1)
    moved_cache = jnp.where(present[:, None, None], arrived[which_move], first_cache)
    second_position = moved_len + 1
    final_cache = insert_token(moved_cache, second_fresh[:, 0], second_position)
    second_out = attend_rows(final_cache, second_position, second_query[:, 0], basis, out_weight)
    return (first_out, second_out, final_cache[:, None])


def solution(mesh):
    placed = (
        P("req", "head", None, None),
        P("req", "head", None),
        P("req", "head", None),
        P("req", "head", None),
        P("req", "head", None),
        P("head", None, None),
        P("head", None),
        P(),
        P(),
        P(),
    )
    return jax.shard_map(
        shards,
        mesh=mesh,
        in_specs=placed,
        out_specs=(P("req", "head"), P("req", "head"), P("req", "head", None, None)),
        check_vma=False,
    )
```

profile of v0, /device:TPU:24, one launch (start us, length us, event | category | flops | bytes accessed | tf_op | source)
XLA Modules:
  0.0 378.1 jit_solution(941315031865206854)
XLA Ops:
  7.2 0.9 dynamic-slice_reduce_fusion
  8.1 0.9 fusion.32
  9.2 1.7 bitcast_select_fusion.1
  10.9 0.6 gather_fusion.1
  11.5 6.8 %gather_fusion.2 = bf16[64,512,192]{1,2,0:T(8,128)(2,1)} fusion(bf16[4,512,192]{1,2,0:T(8,128)(2,1)S(1)} %gather_fusion.1, s32[1024]{0:T(1024)S(1)} %pad_clamp_fusion.2), kind=kCustom, calls=%fused_computation.2 | custom fusion | bytes 25166080 | tf_op jit(solution)/shard_map/gather | solution.py:84
  18.3 14.8 %all-to-all-start = ((bf16[64,512,192]{1,2,0:T(8,128)(2,1)}), bf16[64,512,192]{1,2,0:T(8,128)(2,1)}, u32[]{:S(2)}, u32[]{:S(2)}) async-start(bf16[64,512,192]{1,2,0:T(8,128)(2,1)} %gather_fusion.2), calls=%async_computation.1 | async-start | bytes 25165824 | tf_op jit(solution)/shard_map/all_to_all | solution.py:85
  33.2 0.5 fusion.42
  33.7 0.4 fusion.11
  34.1 5.3 %convolution_convert_fusion.1 = bf16[8,4096]{1,0:T(8,128)(2,1)} fusion(bf16[1024,4096]{1,0:T(8,128)(2,1)} %param.16, bf16[1,8,8,128]{3,2,1,0:T(8,128)(2,1)S(1)} %fusion.11), kind=kOutput, calls=%fused_computation.9 | convolution fusion | flops 67141632 | bytes 8470528 | tf_op jit(solution)/shard_map/dot_general | solution.py:40
  39.9 0.1 reshape.336
  40.0 0.1 eq.91
  40.2 0.2 select_reduce_fusion
  40.4 0.1 reshape.338
  40.6 1.9 gather_fusion
  42.6 1.4 scatter_fusion
  44.4 151.8 %all-to-all-done = bf16[64,512,192]{1,2,0:T(8,128)(2,1)} async-done(((bf16[64,512,192]{1,2,0:T(8,128)(2,1)}), bf16[64,512,192]{1,2,0:T(8,128)(2,1)}, u32[]{:S(2)}, u32[]{:S(2)}) %all-to-all-start) | async-done | bytes 12582944 | tf_op jit(solution)/shard_map/all_to_all | solution.py:85
  196.2 6.0 %gather_fusion.3 = bf16[4,512,192]{1,2,0:T(8,128)(2,1)} fusion(bf16[64,512,192]{1,2,0:T(8,128)(2,1)} %all-to-all-done, s32[1024]{0:T(1024)S(1)} %pad_clamp_fusion.1), kind=kCustom, calls=%fused_computation.3 | custom fusion | bytes 1572880 | tf_op jit(solution)/shard_map/gather | solution.py:87
  202.3 1.9 gather_fusion.4
  204.2 1.5 select_select_fusion
  205.7 1.5 fusion.43
  207.2 1.6 fusion.12
  208.9 5.2 %convolution_convert_fusion = bf16[8,4096]{1,0:T(8,128)(2,1)} fusion(bf16[1024,4096]{1,0:T(8,128)(2,1)} %param.16, bf16[1,8,8,128]{3,2,1,0:T(8,128)(2,1)S(1)} %fusion.12), kind=kOutput, calls=%fused_computation.8 | convolution fusion | flops 67141632 | bytes 8470528 | tf_op jit(solution)/shard_map/dot_general | solution.py:40
  214.1 1.5 fusion.4
  215.6 155.7 %reduce-scatter.5.cloned.1.call-done = bf16[8,1024]{1,0:T(8,128)(2,1)} async-done(((bf16[8,4096]{1,0:T(8,128)(2,1)}), bf16[8,1024]{1,0:T(8,128)(2,1)}) %reduce-scatter.5.cloned.1.call-update) | async-done | bytes 16400 | tf_op jit(solution)/shard_map/reduce_scatter | solution.py:41
  (48 shorter events, 1.3 us)
Async XLA Ops:
  7.2 26.0 %copy-start = (bf16[1,64,128]{2,1,0:T(8,128)(2,1)S(1)}, bf16[1,64,128]{2,1,0:T(8,128)(2,1)}, u32[]{:S(2)}) copy-start(bf16[1,64,128]{2,1,0:T(8,128)(2,1)} %param.15) | copy-start | bytes 49156
  18.3 14.9 %copy-start.7 = (bf16[8,1,1024]{2,0,1:T(8,128)(2,1)S(1)}, bf16[8,1,1024]{2,0,1:T(8,128)(2,1)}, u32[]{:S(2)}) copy-start(bf16[8,1,1024]{2,0,1:T(8,128)(2,1)} %param.13) | copy-start | bytes 49156
  18.3 177.9 %all-to-all-start = ((bf16[64,512,192]{1,2,0:T(8,128)(2,1)}), bf16[64,512,192]{1,2,0:T(8,128)(2,1)}, u32[]{:S(2)}, u32[]{:S(2)}) async-start(bf16[64,512,192]{1,2,0:T(8,128)(2,1)} %gather_fusion.2), calls=%async_computation.1 | async-start | bytes 25165824 | tf_op jit(solution)/shard_map/all_to_all | solution.py:85
  33.1 182.5 %reduce-scatter.3.cloned.1.call-start = ((), (), s32[]{:S(2)}) async-start(), calls=%async_computation.3 | async-start | bytes 81920 | tf_op jit(solution)/shard_map/reduce_scatter | solution.py:41
  34.1 5.4 %copy-start.5 = (s32[64,4]{0,1:T(4,128)S(1)}, s32[64,4]{0,1:T(4,128)}, u32[]{:S(2)}) copy-start(s32[64,4]{0,1:T(4,128)} %param.19) | copy-start | bytes 3076
  34.1 5.5 %copy-start.4 = (s32[64,8]{0,1:T(8,128)S(1)}, s32[64,8]{0,1:T(8,128)}, u32[]{:S(2)}) copy-start(s32[64,8]{0,1:T(8,128)} %param.17) | copy-start | bytes 6148
  34.1 5.5 %copy-start.6 = (s32[64,4]{0,1:T(4,128)S(1)}, s32[64,4]{0,1:T(4,128)}, u32[]{:S(2)}) copy-start(s32[64,4]{0,1:T(4,128)} %param.18) | copy-start | bytes 3076
  39.4 331.9 %reduce-scatter.5.cloned.1.call-start = ((), (), s32[]{:S(2)}) async-start(), calls=%async_computation.4 | async-start | bytes 81920 | tf_op jit(solution)/shard_map/reduce_scatter | solution.py:41
  202.3 1.9 copy-start.1
  202.3 1.9 copy-start.2
  202.3 1.9 copy-start.3
  204.2 1.5 copy-start.8
Sparse Core Ops, SparseCore 0:
  39.5 27.7 reduce-scatter.2
  214.2 156.9 reduce-scatter.4
where the time goes:
time: 379 us; the launch traced here: 378 us
  waiting for transfers between devices  308 us (81%)
  local copies, waits for them, and re-layouts  20.6 us (5%)
  starting transfers between devices  14.9 us (4%)
  matrix products  14.5 us (4%)
  between operations  14.3 us (4%)
  other arithmetic  6.24 us (2%)
    reduce_scatter x2, waiting for transfers between devices, attend_rows(): lax.psum_scatter(partial_value.astype(jnp.bfloat16), 'head', scatter_dime...  156 us
    all_to_all x1, waiting for transfers between devices, shards(): lax.all_to_all(packed, 'req', split_axis=0, concat_axis=0, tiled=True)  152 us
    all_to_all x1, starting transfers between devices, shards(): lax.all_to_all(packed, 'req', split_axis=0, concat_axis=0, tiled=True)  14.8 us
    dot_general x2, matrix products, attend_rows(): jnp.dot(attended, out_weight, preferred_element_type=jnp.float32)  10.5 us
  transfers between devices with their start and end apart: 3, of which 2 were waited for; matrix products, arithmetic and copies ran while one was open for 8% of the time, Pallas kernels for 0%

commit v1 on v0

v1 whole, which is shorter than its diff:
```python
import functools
import math

import jax
import jax.numpy as jnp
from jax import lax
from jax.experimental import pallas as pl
from jax.experimental.pallas import tpu as pltpu
from jax.sharding import PartitionSpec as P

MESH = pl.DeviceIdType.MESH
NT = (((1,), (1,)), ((), ()))
TILES = 48
BF16 = jnp.bfloat16
F32 = jnp.float32


def relay_place(index, head):
    pair = index // 6
    r = lax.rem(index, 6)
    y = pair // 2
    even = lax.rem(y + head, 2)
    main = r < 4
    x = 2 * lax.rem(pair, 2) + jnp.where(main, even, 1 - even)
    z_hi = jnp.where(main, r // 2, r - 4)
    core = jnp.where(main, lax.rem(r, 2), 0)
    return ((y * 2 + z_hi) * 4 + x) * 2 + core


def relay_role(me, head):
    core = lax.rem(me, 2)
    x = lax.rem(me // 2, 4)
    z_hi = lax.rem(me // 8, 2)
    y = me // 16
    pair = y * 2 + x // 2
    main = lax.rem(x, 2) == lax.rem(y + head, 2)
    index = pair * 6 + jnp.where(main, z_hi * 2 + core, 4 + z_hi)
    return jnp.logical_or(main, core == 0), index


def tile_of(q):
    return 16 * (q // 4), 128 * (q % 4)


def spread_columns(fresh):
    wide = fresh.astype(F32)
    rows = [jnp.broadcast_to(wide[s : s + 1], (128, 192)) for s in range(8)]
    rows = jnp.concatenate(rows, axis=0).astype(BF16)
    eye = (
        lax.broadcasted_iota(jnp.int32, (192, 192), 0)
        == lax.broadcasted_iota(jnp.int32, (192, 192), 1)
    ).astype(F32).astype(BF16)
    return lax.dot_general(eye, rows, NT, preferred_element_type=F32).astype(BF16)


def reduce_query(query, basis):
    wide = query.astype(F32)
    rows = jnp.concatenate([wide[:, 128 * q : 128 * q + 128] for q in range(8)], axis=0)
    tiled = jnp.concatenate([basis.astype(F32)] * 8, axis=0).astype(BF16)
    reduced = lax.dot_general(rows.astype(BF16), tiled, NT, preferred_element_type=F32)
    row = lax.broadcasted_iota(jnp.int32, (64, 512), 0)
    lane = lax.broadcasted_iota(jnp.int32, (64, 512), 1)
    return jnp.where(lax.rem(row, 8) == lane // 64, reduced, 0.0).astype(BF16)


def attend(cache, reduced, positions):
    factors = cache[:, 0:64, :].reshape(512, 512)
    scores = jnp.dot(reduced, factors, preferred_element_type=F32) * (1.0 / math.sqrt(128))
    slot = lax.rem(lax.broadcasted_iota(jnp.int32, (64, 512), 0), 8)
    token = lax.broadcasted_iota(jnp.int32, (64, 512), 1)
    limit = jnp.zeros((64, 512), jnp.int32)
    for s in range(8):
        limit = jnp.where(slot == s, positions[s], limit)
    scores = jnp.where(token <= limit, scores, -1e30)
    raw = jnp.exp(scores - jnp.max(scores, axis=-1, keepdims=True))
    weights = raw / jnp.sum(raw, axis=-1, keepdims=True)
    total = jnp.zeros((64, 128), F32)
    for s in range(8):
        own = jnp.where(slot == s, weights, 0.0).astype(BF16)
        total = total + lax.dot_general(
            own, cache[s, 64:192, :], NT, preferred_element_type=F32
        )
    return jnp.concatenate([total[8 * q : 8 * q + 8] for q in range(8)], axis=1).astype(BF16)


def project(attended, weight, share):
    def block(t, carry):
        start = pl.multiple_of(t * 1024, 1024)
        low = jnp.dot(attended, weight[:, pl.ds(start, 512)], preferred_element_type=F32)
        high = jnp.dot(attended, weight[:, pl.ds(start + 512, 512)], preferred_element_type=F32)
        share[t] = jnp.concatenate([low, high], axis=0).astype(BF16)
        return carry

    lax.fori_loop(0, 4, block, 0)


def kernel(
    leave, arrive, lens, leave_v, kv_hbm, ff, sf, q1, q2, basis, w_hbm,
    out1, out2, cache_hbm,
    kv, w, fin, s1, r1, s2, r2, tab_v, tab, cols, share1, share2, got1, got2,
    local_sem, send_sem, recv_sem, share_send, share_recv,
):
    me = lax.axis_index("req")
    head = lax.axis_index("head")
    across = lax.rem(head + 2, 4)
    is_relay, relay = relay_role(me, head)

    load_kv = pltpu.make_async_copy(kv_hbm, kv, local_sem.at[0])
    load_kv.start()
    load_w = pltpu.make_async_copy(w_hbm, w, local_sem.at[1])
    load_w.start()

    barrier = pltpu.get_barrier_semaphore()

    def greet(k, carry):
        pl.semaphore_signal(
            barrier, inc=1, device_id=(lax.rem(me + k, 64), across), device_id_type=MESH
        )
        return carry

    lax.fori_loop(0, 64, greet, 0)
    for d in (1, 3):
        pl.semaphore_signal(
            barrier, inc=1, device_id=(me, lax.rem(head + d, 4)), device_id_type=MESH
        )

    lane = lax.broadcasted_iota(jnp.int32, (16, 128), 1)
    p1 = [lens[s, me] for s in range(8)]
    cols[...] = spread_columns(ff[...])
    load_kv.wait()
    for s in range(8):
        for v in range(4):
            hit = lane + 128 * v == p1[s]
            for u in range(12):
                at = (s, pl.ds(16 * u, 16), pl.ds(128 * v, 128))
                fresh = cols[pl.ds(16 * u, 16), pl.ds(128 * s, 128)]
                kv[at] = jnp.where(hit, fresh.astype(F32), kv[at].astype(F32)).astype(BF16)
    for m in range(4):
        row = leave[m, me]
        for q in range(TILES):
            a, b = tile_of(q)
            s1[q, m] = kv[row, a : a + 16, b : b + 128]

    pl.semaphore_wait(barrier, 66)

    def spread(k, carry):
        q = lax.rem(k + me, TILES)
        pltpu.make_async_remote_copy(
            src_ref=s1.at[q], dst_ref=r1.at[me], send_sem=send_sem.at[0], recv_sem=recv_sem.at[0],
            device_id=(relay_place(q, head), across), device_id_type=MESH,
        ).start()
        return carry

    lax.fori_loop(0, TILES, spread, 0)

    place = 8 * lax.broadcasted_iota(jnp.int32, (4, 64), 1) + leave_v[...]

    def look(g, found):
        for m in range(4):
            found = jnp.where(place == arrive[m, g], 4 * g + m, found)
        return found

    tab_v[...] = lax.fori_loop(0, 64, look, jnp.zeros((4, 64), jnp.int32))
    copy_tab = pltpu.make_async_copy(tab_v, tab, local_sem.at[2])
    copy_tab.start()

    def share_out(share, got, which):
        for d in (1, 2, 3):
            to = lax.rem(head + d, 4)
            pltpu.make_async_remote_copy(
                src_ref=share.at[to], dst_ref=got.at[d - 1], send_sem=share_send.at[which],
                recv_sem=share_recv.at[which], device_id=(me, to), device_id_type=MESH,
            ).start()

    def share_in(share, got, which, out):
        pltpu.make_async_copy(got, got, share_recv.at[which]).wait()
        total = share[head].astype(F32)
        for d in range(3):
            total = total + got[d].astype(F32)
        out[...] = jnp.concatenate([total[0:8], total[8:16]], axis=1).astype(BF16)
        pltpu.make_async_copy(got, got, share_send.at[which]).wait()

    attended1 = attend(kv, reduce_query(q1[...], basis[...]), p1)
    load_w.wait()
    project(attended1, w, share1)
    share_out(share1, got1, 0)
    cols[...] = spread_columns(sf[...])
    reduced2 = reduce_query(q2[...], basis[...])

    copy_tab.wait()
    pltpu.make_async_copy(s1, s1, send_sem.at[0]).wait()

    @pl.when(is_relay)
    def _():
        pltpu.make_async_copy(r1, r1, recv_sem.at[0]).wait()

        def pick(j, carry):
            for a in range(4):
                s2[j, a] = r1[tab[a, j] // 4, lax.rem(tab[a, j], 4)]
            return carry

        lax.fori_loop(0, 64, pick, 0)

        def deliver(k, carry):
            j = lax.rem(k + me, 64)
            pltpu.make_async_remote_copy(
                src_ref=s2.at[j], dst_ref=r2.at[relay], send_sem=send_sem.at[1],
                recv_sem=recv_sem.at[1], device_id=(j, across), device_id_type=MESH,
            ).start()
            return carry

        lax.fori_loop(0, 64, deliver, 0)

    share_in(share1, got1, 0, out1)
    pltpu.make_async_copy(r2, r2, recv_sem.at[1]).wait()

    p2 = []
    stores = []
    for s in range(8):
        come = jnp.int32(0)
        stay = jnp.int32(1)
        for a in range(4):
            here = leave[a, me] == s
            come = jnp.where(here, a, come)
            stay = jnp.where(here, 0, stay)
        source = tab[come, me]
        group = source // 4
        length = jnp.where(stay == 1, p1[s], lens[leave[lax.rem(source, 4), group], group]) + 1
        p2.append(length)
        kept = jnp.full((16, 128), stay, jnp.int32) == 1
        for q in range(TILES):
            a, b = tile_of(q)
            tile = jnp.where(kept, kv[s, a : a + 16, b : b + 128].astype(F32), r2[q, come].astype(F32))
            fresh = cols[a : a + 16, 128 * s : 128 * s + 128].astype(F32)
            fin[s, a : a + 16, b : b + 128] = jnp.where(lane + b == length, fresh, tile).astype(BF16)
        store = pltpu.make_async_copy(fin.at[s], cache_hbm.at[s], local_sem.at[3 + s])
        store.start()
        stores.append(store)

    project(attend(fin, reduced2, p2), w, share2)
    share_out(share2, got2, 1)
    share_in(share2, got2, 1, out2)
    for store in stores:
        store.wait()

    @pl.when(is_relay)
    def _():
        pltpu.make_async_copy(s2, s2, send_sem.at[1]).wait()


def shards(
    kv_cache, first_fresh, second_fresh, first_query, second_query, key_basis, out_weight,
    lengths, leave_slot, arrive_row,
):
    kv = kv_cache[:, 0].transpose(0, 2, 1)
    smem = pl.BlockSpec(memory_space=pltpu.SMEM)
    vmem = pl.BlockSpec(memory_space=pltpu.VMEM)
    anywhere = pl.BlockSpec(memory_space=pl.ANY)
    out1, out2, cache = pl.pallas_call(
        kernel,
        out_shape=(
            jax.ShapeDtypeStruct((8, 1024), BF16),
            jax.ShapeDtypeStruct((8, 1024), BF16),
            jax.ShapeDtypeStruct((8, 192, 512), BF16),
        ),
        in_specs=[smem, smem, smem, vmem, anywhere] + [vmem] * 5 + [anywhere],
        out_specs=(vmem, vmem, anywhere),
        scratch_shapes=[
            pltpu.VMEM((8, 192, 512), BF16),
            pltpu.VMEM((1024, 4096), BF16),
            pltpu.VMEM((8, 192, 512), BF16),
            pltpu.VMEM((TILES, 4, 16, 128), BF16),
            pltpu.VMEM((64, 4, 16, 128), BF16),
            pltpu.VMEM((64, 4, 16, 128), BF16),
            pltpu.VMEM((TILES, 4, 16, 128), BF16),
            pltpu.VMEM((4, 64), jnp.int32),
            pltpu.SMEM((4, 64), jnp.int32),
            pltpu.VMEM((192, 1024), BF16),
            pltpu.VMEM((4, 16, 512), BF16),
            pltpu.VMEM((4, 16, 512), BF16),
            pltpu.VMEM((3, 16, 512), BF16),
            pltpu.VMEM((3, 16, 512), BF16),
            pltpu.SemaphoreType.DMA((11,)),
            pltpu.SemaphoreType.DMA((2,)),
            pltpu.SemaphoreType.DMA((2,)),
            pltpu.SemaphoreType.DMA((2,)),
            pltpu.SemaphoreType.DMA((2,)),
        ],
        compiler_params=pltpu.CompilerParams(
            collective_id=0, has_side_effects=True, vmem_limit_bytes=48 * 1024 * 1024
        ),
    )(
        leave_slot.T, arrive_row.T, lengths.T, leave_slot.T, kv,
        first_fresh[:, 0], second_fresh[:, 0], first_query[:, 0], second_query[:, 0],
        key_basis[0], out_weight,
    )
    return out1, out2, cache.transpose(0, 2, 1)[:, None]


def solution(mesh):
    placed = (
        P("req", "head", None, None),
        P("req", "head", None),
        P("req", "head", None),
        P("req", "head", None),
        P("req", "head", None),
        P("head", None, None),
        P("head", None),
        P(),
        P(),
        P(),
    )
    return jax.shard_map(
        shards,
        mesh=mesh,
        in_specs=placed,
        out_specs=(P("req", "head"), P("req", "head"), P("req", "head", None, None)),
        check_vma=False,
    )
```

time: 379 us -> 75.7 us (0.20)
  waiting for transfers between devices: 308 us -> 0 us
  Pallas kernels: 0 us -> 64.6 us
  starting transfers between devices: 14.9 us -> 0 us
  matrix products: 14.5 us -> 0 us
  between operations: 14.3 us -> 0.66 us
  local copies, waits for them, and re-layouts: 20.6 us -> 9.33 us
  other arithmetic: 6.24 us -> 0 us
    reduce_scatter x2 -> x0, waiting for transfers between devices: 156 us -> none  [attend_rows(): lax.psum_scatter(partial_value.astype(jnp.bfloat16), 'head', scatter_dime...]
    all_to_all x1 -> x0, waiting for transfers between devices: 152 us -> none  [shards(): lax.all_to_all(packed, 'req', split_axis=0, concat_axis=0, tiled=True)]
    pallas_call x0 -> x1, Pallas kernels: none -> 64.6 us  [shards(): pl.pallas_call(kernel, out_shape=(jax.ShapeDtypeStruct((8, 1024), BF16),...]
    gather x5 -> x0, local copies, waits for them, and re-layouts: 17.3 us -> none  [the longest x1 6.81 us: shards(): packed = outgoing[chosen]]
    all_to_all x1 -> x0, starting transfers between devices: 14.8 us -> none  [shards(): lax.all_to_all(packed, 'req', split_axis=0, concat_axis=0, tiled=True)]
    dot_general x4 -> x0, matrix products: 12.5 us -> none  [the longest x2 10.5 us: attend_rows(): jnp.dot(attended, out_weight, preferred_element_type=jnp.float32)]
    unnamed x20 -> x21, local copies, waits for them, and re-layouts: 0.22 us -> 9.33 us
    select_n x8 -> x0, other arithmetic: 4.12 us -> none  [the longest x2 3.15 us: insert_token(): return jnp.where(hit_mask, fresh_rows[:, None, :], cache_rows)]
  transfers between devices with their start and end apart: 3 -> 0, of which waited for: 2 -> 0; matrix products, arithmetic and copies ran while one was open for 8% -> 0% of each run, Pallas kernels for 0% -> 0%
where the time goes in v1:
time: 75.7 us; the launch traced here: 74.6 us
  Pallas kernels  64.6 us (85%)
  local copies, waits for them, and re-layouts  9.33 us (12%)
    pallas_call x1, Pallas kernels, shards(): pl.pallas_call(kernel, out_shape=(jax.ShapeDtypeStruct((8, 1024), BF16),...  64.6 us
    unnamed x21, local copies, waits for them, and re-layouts  9.33 us

profile of v1, /device:TPU:24, one launch (start us, length us, event | category | flops | bytes accessed | tf_op | source)
XLA Modules:
  0.0 74.6 jit_solution(9537956940322036109)
XLA Ops:
  0.6 0.0 copy-start
  0.6 1.4 %copy-done = bf16[8,1,512,192]{2,3,1,0:T(8,128)(2,1)S(1)} copy-done((bf16[8,1,512,192]{2,3,1,0:T(8,128)(2,1)S(1)}, bf16[8,1,512,192]{2,3,1,0:T(8,128)(2,1)}, u32[]{:S(2)}) %copy-start) | copy-done | bytes 1572888
  2.0 0.0 copy-start.1
  2.0 0.7 copy-done.1
  2.8 0.0 copy-start.2
  2.8 0.7 copy-done.2
  3.5 0.0 copy-start.3
  3.5 0.7 copy-done.3
  4.2 0.0 copy-start.4
  4.2 0.7 copy-done.4
  4.9 0.0 copy-start.5
  4.9 0.7 copy-done.5
  5.6 0.0 copy-start.6
  5.6 0.7 copy-done.6
  6.3 0.0 copy-start.7
  6.3 0.7 copy-done.7
  6.9 0.0 copy-start.8
  6.9 0.7 copy-done.8
  7.6 64.6 %shard_map.121 = (bf16[8,1024]{1,0:T(8,128)(2,1)S(1)}, bf16[8,1024]{1,0:T(8,128)(2,1)S(1)}, bf16[8,192,512]{2,1,0:T(8,128)(2,1)S(1)}) custom-call(s32[4,64]{1,0:T(4,128)S(1)} %bitcast.21, s32[4,64]{1,0:T(4,128)S(1)} %bitcast.26, s32[8,64]{1,0:T(8,128)S(1)} %bitcast.23, s32[4,64]{1,0:T(4,128)S(1)} %bitcast.22, bf16[8,192,512]{2,1,0:T(8,128)(2,1)S(1)} %bitcast.17, ...), custom_call_target="tpu_custom_call" | custom-call | tf_op jit(solution)/shard_map/pallas_call | solution.py:259
  72.3 0.6 copy.17
  72.9 0.6 copy.18
  73.5 1.1 %copy.19 = bf16[8,1,512,192]{2,3,1,0:T(8,128)(2,1)} copy(bf16[8,1,512,192]{2,3,1,0:T(8,128)(2,1)S(1)} %bitcast.16) | data formatting | bytes 3145728
Async XLA Ops:
  0.6 1.4 %copy-start = (bf16[8,1,512,192]{2,3,1,0:T(8,128)(2,1)S(1)}, bf16[8,1,512,192]{2,3,1,0:T(8,128)(2,1)}, u32[]{:S(2)}) copy-start(bf16[8,1,512,192]{2,3,1,0:T(8,128)(2,1)} %param.10) | copy-start | bytes 4718596
  2.0 0.7 copy-start.1
  2.8 0.7 copy-start.2
  3.5 0.7 copy-start.3
  4.2 0.7 copy-start.4
  4.9 0.7 copy-start.5
  5.6 0.7 copy-start.6
  6.3 0.7 copy-start.7
  6.9 0.7 copy-start.8

commit v2 on v1

--- a/solution.py
+++ b/solution.py
@@ -13,6 +13,13 @@
 TILES = 48
 BF16 = jnp.bfloat16
 F32 = jnp.float32
+
+
+def hops(k):
+    return (0, 1, 2, 1)[k // 16] + (0, 1, 2, 1)[k // 2 % 4]
+
+
+FAR_FIRST = sorted(range(64), key=lambda k: (-hops(k), k))
 
 
 def relay_place(index, head):
@@ -95,9 +102,9 @@
 
 
 def kernel(
-    leave, arrive, lens, leave_v, kv_hbm, ff, sf, q1, q2, basis, w_hbm,
-    out1, out2, cache_hbm,
-    kv, w, fin, s1, r1, s2, r2, tab_v, tab, cols, share1, share2, got1, got2,
+    leave_hbm, arrive_hbm, lens_hbm, kv_hbm, ff_hbm, sf_hbm, q1_hbm, q2_hbm, basis_hbm, w_hbm,
+    out1_hbm, out2_hbm, cache_hbm,
+    out1, out2, fin, leave, arrive, lens, leave_v, ff, sf, q1, q2, basis, kv, w, s1, r1, s2, r2, tab_v, tab, cols, share1, share2, got1, got2,
     local_sem, send_sem, recv_sem, share_send, share_recv,
 ):
     me = lax.axis_index("req")
@@ -105,29 +112,44 @@
     across = lax.rem(head + 2, 4)
     is_relay, relay = relay_role(me, head)
 
-    load_kv = pltpu.make_async_copy(kv_hbm, kv, local_sem.at[0])
-    load_kv.start()
-    load_w = pltpu.make_async_copy(w_hbm, w, local_sem.at[1])
-    load_w.start()
+    loads = [
+        pltpu.make_async_copy(source, target, local_sem.at[i])
+        for i, (source, target) in enumerate(
+            (
+                (lens_hbm, lens),
+                (leave_hbm, leave),
+                (ff_hbm, ff),
+                (kv_hbm, kv),
+                (arrive_hbm, arrive),
+                (leave_hbm, leave_v),
+                (q1_hbm, q1),
+                (basis_hbm, basis),
+                (q2_hbm, q2),
+                (sf_hbm, sf),
+                (w_hbm, w),
+            )
+        )
+    ]
+    for load in loads:
+        load.start()
 
     barrier = pltpu.get_barrier_semaphore()
 
-    def greet(k, carry):
+    for k in FAR_FIRST:
         pl.semaphore_signal(
-            barrier, inc=1, device_id=(lax.rem(me + k, 64), across), device_id_type=MESH
+            barrier, inc=1, device_id=(jnp.bitwise_xor(me, k), across), device_id_type=MESH
         )
-        return carry
-
-    lax.fori_loop(0, 64, greet, 0)
     for d in (1, 3):
         pl.semaphore_signal(
             barrier, inc=1, device_id=(me, lax.rem(head + d, 4)), device_id_type=MESH
         )
 
     lane = lax.broadcasted_iota(jnp.int32, (16, 128), 1)
+    for load in loads[:3]:
+        load.wait()
     p1 = [lens[s, me] for s in range(8)]
     cols[...] = spread_columns(ff[...])
-    load_kv.wait()
+    loads[3].wait()
     for s in range(8):
         for v in range(4):
             hit = lane + 128 * v == p1[s]
@@ -153,6 +175,9 @@
 
     lax.fori_loop(0, TILES, spread, 0)
 
+    for load in loads[4:10]:
+        load.wait()
+
     place = 8 * lax.broadcasted_iota(jnp.int32, (4, 64), 1) + leave_v[...]
 
     def look(g, found):
@@ -161,7 +186,7 @@
         return found
 
     tab_v[...] = lax.fori_loop(0, 64, look, jnp.zeros((4, 64), jnp.int32))
-    copy_tab = pltpu.make_async_copy(tab_v, tab, local_sem.at[2])
+    copy_tab = pltpu.make_async_copy(tab_v, tab, local_sem.at[11])
     copy_tab.start()
 
     def share_out(share, got, which):
@@ -181,7 +206,7 @@
         pltpu.make_async_copy(got, got, share_send.at[which]).wait()
 
     attended1 = attend(kv, reduce_query(q1[...], basis[...]), p1)
-    load_w.wait()
+    loads[10].wait()
     project(attended1, w, share1)
     share_out(share1, got1, 0)
     cols[...] = spread_columns(sf[...])
@@ -215,7 +240,6 @@
     pltpu.make_async_copy(r2, r2, recv_sem.at[1]).wait()
 
     p2 = []
-    stores = []
     for s in range(8):
         come = jnp.int32(0)
         stay = jnp.int32(1)
@@ -233,19 +257,38 @@
             tile = jnp.where(kept, kv[s, a : a + 16, b : b + 128].astype(F32), r2[q, come].astype(F32))
             fresh = cols[a : a + 16, 128 * s : 128 * s + 128].astype(F32)
             fin[s, a : a + 16, b : b + 128] = jnp.where(lane + b == length, fresh, tile).astype(BF16)
-        store = pltpu.make_async_copy(fin.at[s], cache_hbm.at[s], local_sem.at[3 + s])
+
+    stores = [
+        pltpu.make_async_copy(out1, out1_hbm, local_sem.at[12]),
+        pltpu.make_async_copy(fin, cache_hbm, local_sem.at[13]),
+    ]
+    for store in stores:
         store.start()
-        stores.append(store)
-
     project(attend(fin, reduced2, p2), w, share2)
     share_out(share2, got2, 1)
     share_in(share2, got2, 1, out2)
+    stores.append(pltpu.make_async_copy(out2, out2_hbm, local_sem.at[14]))
+    stores[2].start()
     for store in stores:
         store.wait()
 
     @pl.when(is_relay)
     def _():
         pltpu.make_async_copy(s2, s2, send_sem.at[1]).wait()
+
+
+def hand_over(out1, out2, cache, to1, to2, to_cache, held, held1, held2, sem_in, sem_out):
+    ways = [(cache.at[s], held.at[s], to_cache.at[s]) for s in range(8)]
+    ways += [(out1, held1, to1), (out2, held2, to2)]
+    come = [pltpu.make_async_copy(a, b, sem_in.at[i]) for i, (a, b, c) in enumerate(ways)]
+    go = [pltpu.make_async_copy(b, c, sem_out.at[i]) for i, (a, b, c) in enumerate(ways)]
+    for copy in come:
+        copy.start()
+    for first, second in zip(come, go):
+        first.wait()
+        second.start()
+    for copy in go:
+        copy.wait()
 
 
 def shards(
@@ -253,9 +296,7 @@
     lengths, leave_slot, arrive_row,
 ):
     kv = kv_cache[:, 0].transpose(0, 2, 1)
-    smem = pl.BlockSpec(memory_space=pltpu.SMEM)
-    vmem = pl.BlockSpec(memory_space=pltpu.VMEM)
-    anywhere = pl.BlockSpec(memory_space=pl.ANY)
+    hbm = pl.BlockSpec(memory_space=pltpu.HBM)
     out1, out2, cache = pl.pallas_call(
         kernel,
         out_shape=(
@@ -263,12 +304,23 @@
             jax.ShapeDtypeStruct((8, 1024), BF16),
             jax.ShapeDtypeStruct((8, 192, 512), BF16),
         ),
-        in_specs=[smem, smem, smem, vmem, anywhere] + [vmem] * 5 + [anywhere],
-        out_specs=(vmem, vmem, anywhere),
+        in_specs=[hbm] * 10,
+        out_specs=(hbm, hbm, hbm),
         scratch_shapes=[
+            pltpu.VMEM((8, 1024), BF16),
+            pltpu.VMEM((8, 1024), BF16),
+            pltpu.VMEM((8, 192, 512), BF16),
+            pltpu.SMEM((4, 64), jnp.int32),
+            pltpu.SMEM((4, 64), jnp.int32),
+            pltpu.SMEM((8, 64), jnp.int32),
+            pltpu.VMEM((4, 64), jnp.int32),
+            pltpu.VMEM((8, 192), BF16),
+            pltpu.VMEM((8, 192), BF16),
+            pltpu.VMEM((8, 1024), BF16),
+            pltpu.VMEM((8, 1024), BF16),
+            pltpu.VMEM((64, 128), BF16),
             pltpu.VMEM((8, 192, 512), BF16),
             pltpu.VMEM((1024, 4096), BF16),
-            pltpu.VMEM((8, 192, 512), BF16),
             pltpu.VMEM((TILES, 4, 16, 128), BF16),
             pltpu.VMEM((64, 4, 16, 128), BF16),
             pltpu.VMEM((64, 4, 16, 128), BF16),
@@ -280,20 +332,32 @@
             pltpu.VMEM((4, 16, 512), BF16),
             pltpu.VMEM((3, 16, 512), BF16),
             pltpu.VMEM((3, 16, 512), BF16),
-            pltpu.SemaphoreType.DMA((11,)),
+            pltpu.SemaphoreType.DMA((15,)),
             pltpu.SemaphoreType.DMA((2,)),
             pltpu.SemaphoreType.DMA((2,)),
             pltpu.SemaphoreType.DMA((2,)),
             pltpu.SemaphoreType.DMA((2,)),
         ],
         compiler_params=pltpu.CompilerParams(
-            collective_id=0, has_side_effects=True, vmem_limit_bytes=48 * 1024 * 1024
+            collective_id=0, has_side_effects=True, vmem_limit_bytes=60 * 1024 * 1024
         ),
     )(
-        leave_slot.T, arrive_row.T, lengths.T, leave_slot.T, kv,
+        leave_slot.T, arrive_row.T, lengths.T, kv,
         first_fresh[:, 0], second_fresh[:, 0], first_query[:, 0], second_query[:, 0],
         key_basis[0], out_weight,
     )
+    out1, out2, cache = pl.pallas_call(
+        hand_over,
+        out_shape=(
+            jax.ShapeDtypeStruct((8, 1024), BF16),
+            jax.ShapeDtypeStruct((8, 1024), BF16),
+            jax.ShapeDtypeStruct((8, 192, 512), BF16),
+        ),
+        in_specs=[hbm] * 3,
+        out_specs=(hbm, hbm, hbm),
+        scratch_shapes=[pltpu.VMEM((8, 192, 512), BF16), pltpu.VMEM((8, 1024), BF16), pltpu.VMEM((8, 1024), BF16), pltpu.SemaphoreType.DMA((10,)), pltpu.SemaphoreType.DMA((10,))],
+        compiler_params=pltpu.CompilerParams(vmem_limit_bytes=60 * 1024 * 1024),
+    )(out1, out2, cache)
     return out1, out2, cache.transpose(0, 2, 1)[:, None]
 
 

time: 75.7 us -> 64.9 us (0.86)
  local copies, waits for them, and re-layouts: 9.33 us -> 0 us
  Pallas kernels: 64.6 us -> 63.5 us
    unnamed x21 -> x0, local copies, waits for them, and re-layouts: 9.33 us -> none
    pallas_call x1, Pallas kernels: 64.6 us -> 61.1 us  [shards(): pl.pallas_call(kernel, out_shape=(jax.ShapeDtypeStruct((8, 1024), BF16),...]
    pallas_call x0 -> x1, Pallas kernels: none -> 2.33 us  [shards(): pl.pallas_call(hand_over, out_shape=(jax.ShapeDtypeStruct((8, 1024), BF16...]
where the time goes in v2:
time: 64.9 us; the launch traced here: 64.1 us
  Pallas kernels  63.5 us (98%)
    pallas_call x1, Pallas kernels, shards(): pl.pallas_call(kernel, out_shape=(jax.ShapeDtypeStruct((8, 1024), BF16),...  61.1 us
    pallas_call x1, Pallas kernels, shards(): pl.pallas_call(hand_over, out_shape=(jax.ShapeDtypeStruct((8, 1024), BF16...  2.33 us

profile of v2, /device:TPU:24, one launch (start us, length us, event | category | flops | bytes accessed | tf_op | source)
XLA Modules:
  0.0 64.1 jit_solution(12585657050247399833)
XLA Ops:
  0.6 61.1 %shard_map.121 = (bf16[8,1024]{1,0:T(8,128)(2,1)}, bf16[8,1024]{1,0:T(8,128)(2,1)}, bf16[8,192,512]{2,1,0:T(8,128)(2,1)}) custom-call(s32[4,64]{1,0:T(4,128)} %bitcast.23, s32[4,64]{1,0:T(4,128)} %bitcast.24, s32[8,64]{1,0:T(8,128)} %bitcast.20, bf16[8,192,512]{2,1,0:T(8,128)(2,1)} %bitcast.16, bf16[8,192]{1,0:T(8,128)(2,1)} %bitcast.21, ...), custom_call_target="tpu_custom_call" | custom-call | tf_op jit(solution)/shard_map/pallas_call | solution.py:300
  61.8 2.3 %shard_map.122 = (bf16[8,1024]{1,0:T(8,128)(2,1)}, bf16[8,1024]{1,0:T(8,128)(2,1)}, bf16[8,192,512]{2,1,0:T(8,128)(2,1)}) custom-call(bf16[8,1024]{1,0:T(8,128)(2,1)} %get-tuple-element.9.out1, bf16[8,1024]{1,0:T(8,128)(2,1)} %get-tuple-element.10.out2, bf16[8,192,512]{2,1,0:T(8,128)(2,1)} %get-tuple-element.11.cache), custom_call_target="tpu_custom_call" | custom-call | tf_op jit(solution)/shard_map/pallas_call | solution.py:349

commit v3 on v2

--- a/solution.py
+++ b/solution.py
@@ -11,6 +11,8 @@
 MESH = pl.DeviceIdType.MESH
 NT = (((1,), (1,)), ((), ()))
 TILES = 48
+CROSS = 76
+CROSS_PARTS = 2
 BF16 = jnp.bfloat16
 F32 = jnp.float32
 
@@ -20,6 +22,7 @@
 
 
 FAR_FIRST = sorted(range(64), key=lambda k: (-hops(k), k))
+NEAR_FAR_FIRST = sorted(range(1, 32), key=lambda k: (-hops((k // 8) * 16 + k % 8), k))
 
 
 def relay_place(index, head):
@@ -101,7 +104,7 @@
     lax.fori_loop(0, 4, block, 0)
 
 
-def kernel(
+def general_kernel(
     leave_hbm, arrive_hbm, lens_hbm, kv_hbm, ff_hbm, sf_hbm, q1_hbm, q2_hbm, basis_hbm, w_hbm,
     out1_hbm, out2_hbm, cache_hbm,
     out1, out2, fin, leave, arrive, lens, leave_v, ff, sf, q1, q2, basis, kv, w, s1, r1, s2, r2, tab_v, tab, cols, share1, share2, got1, got2,
@@ -277,6 +280,365 @@
         pltpu.make_async_copy(s2, s2, send_sem.at[1]).wait()
 
 
+def near_place(q, core, me, head):
+    y = jnp.where(q == 12, 0, q // 3)
+    k = jnp.where(q == 12, -1, lax.rem(q, 3))
+    x = lax.rem(9 + core + k - y - head, 4)
+    return y * 16 + lax.rem(me // 8, 2) * 8 + x * 2 + core
+
+
+def group_at(plane, half):
+    return (plane // 8) * 16 + half * 8 + lax.rem(plane, 8)
+
+
+def fast_kernel(
+    leave_hbm, arrive_hbm, lens_hbm, kv_hbm, ff_hbm, sf_hbm, q1_hbm, q2_hbm, basis_hbm, w_hbm,
+    out1_hbm, out2_hbm, cache_hbm, fits,
+    out1, out2, fin, leave, arrive, lens, leave_v, ff, sf, q1, q2, basis, kv, w,
+    ft, s1, ra, rb, xs, both_a, both_b, s2, r2, r3, code_v, source_v, cross_v, code, source, cross,
+    cols, cols1, share1, share2, got1, got2,
+    local_sem, send_a, recv_a, send_b, recv_b, send_c, recv_c, share_send, share_recv,
+):
+    me = lax.axis_index("req")
+    head = lax.axis_index("head")
+    core = lax.rem(me, 2)
+    x = lax.rem(me // 2, 4)
+    half = lax.rem(me // 8, 2)
+    y = me // 16
+    plane = y * 8 + x * 2 + core
+    turn = lax.rem(x + y + head + 3 * core, 4)
+    is_fresh = jnp.logical_and(turn == 0, jnp.logical_and(y == 0, core == 0))
+    is_relay1 = turn != 0
+    is_relay0 = jnp.logical_or(is_relay1, is_fresh)
+    my_q = jnp.where(turn == 0, 0, 3 * y + turn - 1)
+    partner = jnp.bitwise_xor(me, 8)
+
+    barrier = pltpu.get_barrier_semaphore()
+    pl.semaphore_signal(barrier, inc=1, device_id=(partner, head), device_id_type=MESH)
+    for k in NEAR_FAR_FIRST:
+        to = jnp.bitwise_xor(me, (k // 8) * 16 + k % 8)
+        pl.semaphore_signal(barrier, inc=1, device_id=(to, head), device_id_type=MESH)
+    for d in (1, 2, 3):
+        pl.semaphore_signal(
+            barrier, inc=1, device_id=(me, lax.rem(head + d, 4)), device_id_type=MESH
+        )
+
+    loads = [
+        pltpu.make_async_copy(origin, target, local_sem.at[i])
+        for i, (origin, target) in enumerate(
+            (
+                (lens_hbm, lens),
+                (leave_hbm, leave),
+                (ff_hbm, ff),
+                (kv_hbm, kv),
+                (arrive_hbm, arrive),
+                (leave_hbm, leave_v),
+                (q1_hbm, q1),
+                (basis_hbm, basis),
+                (q2_hbm, q2),
+                (sf_hbm, sf),
+                (w_hbm, w),
+            )
+        )
+    ]
+    for load in loads:
+        load.start()
+
+    def post(src, dst, send, recv, to):
+        @pl.when(to != me)
+        def _():
+            pltpu.make_async_remote_copy(
+                src_ref=src, dst_ref=dst, send_sem=send, recv_sem=recv,
+                device_id=(to, head), device_id_type=MESH,
+            ).start()
+
+        @pl.when(to == me)
+        def _():
+            pltpu.make_async_copy(src, dst, recv).start()
+
+    def drain(ref, sem):
+        pltpu.make_async_copy(ref, ref, sem).wait()
+
+    lane = lax.broadcasted_iota(jnp.int32, (16, 128), 1)
+    for load in loads[:3]:
+        load.wait()
+    p1 = [lens[s, me] for s in range(8)]
+    cols[...] = spread_columns(ff[...])
+    wide = ff[...].astype(F32)
+    for s in range(8):
+        low = wide[s : s + 1, 0:128]
+        high = jnp.concatenate([wide[s : s + 1, 128:192], jnp.zeros((1, 64), F32)], axis=1)
+        ft[s] = jnp.concatenate([low, high, jnp.zeros((14, 128), F32)], axis=0).astype(BF16)
+    loads[3].wait()
+    for s in range(8):
+        for v in range(4):
+            hit = lane + 128 * v == p1[s]
+            for u in range(12):
+                at = (s, pl.ds(16 * u, 16), pl.ds(128 * v, 128))
+                fresh = cols[pl.ds(16 * u, 16), pl.ds(128 * s, 128)]
+                kv[at] = jnp.where(hit, fresh.astype(F32), kv[at].astype(F32)).astype(BF16)
+
+    rows = [leave[m, me] for m in range(4)]
+    for m in range(4):
+        s1[48, m] = ft[rows[m]]
+    pl.semaphore_wait(barrier, 35)
+
+    mine = pl.ds(4 * plane, 4)
+    post(s1.at[48], ra.at[mine], send_a.at[0], recv_a.at[0], near_place(12, 0, me, head))
+    def spread_tokens(v):
+        landing = ra if v < 2 else rb
+
+        def spread(k, carry):
+            q = lax.rem(k + 3 * y + x, 12)
+            for m in range(4):
+                s1[12 * v + q, m] = kv[
+                    rows[m], pl.ds(pl.multiple_of(16 * q, 16), 16), 128 * v : 128 * v + 128
+                ]
+            post(
+                s1.at[12 * v + q], landing.at[mine], send_a.at[0], recv_a.at[v // 2],
+                near_place(q, v % 2, me, head),
+            )
+            return carry
+
+        lax.fori_loop(0, 12, spread, 0)
+
+    spread_tokens(0)
+    spread_tokens(1)
+    for load in loads[4:10]:
+        load.wait()
+
+    place = 8 * lax.broadcasted_iota(jnp.int32, (4, 64), 1) + leave_v[...]
+    lane_row = lax.broadcasted_iota(jnp.int32, (8, 128), 1)
+    empty = jnp.zeros((4, 64), jnp.int32)
+    carry = (empty, empty, jnp.full((8, 128), 0, jnp.int32))
+    counts = []
+    for side in range(2):
+
+        def look(i, state, side=side):
+            codes, sources, crosses, count = state
+            group = group_at(i, side)
+            for m in range(4):
+                target = arrive[m, group]
+                leaves = jnp.where(lax.rem(target // 64, 2) == side, 0, 1)
+                index = 4 * i + m
+                here = place == target
+                codes = jnp.where(here, jnp.where(leaves == 1, 128 + count, index), codes)
+                sources = jnp.where(here, 4 * group + m, sources)
+                slot = jnp.where(jnp.logical_and(leaves == 1, half == side), count, -1)
+                crosses = jnp.where(lane_row == slot, index, crosses)
+                count = count + leaves
+            return codes, sources, crosses, count
+
+        *carry, count = lax.fori_loop(0, 32, look, (*carry, jnp.int32(0)))
+        counts.append(count)
+    code_v[...], source_v[...], cross_v[...] = carry
+    code_v[...] = jnp.clip(code_v[...], 0, 127 + CROSS)
+    tables = [
+        pltpu.make_async_copy(code_v, code, local_sem.at[11]),
+        pltpu.make_async_copy(source_v, source, local_sem.at[12]),
+        pltpu.make_async_copy(cross_v, cross, local_sem.at[13]),
+    ]
+    stores = []
+    fits[0, 0] = jnp.where(jnp.maximum(counts[0], counts[1]) <= CROSS, 1, 0)
+    for copy in tables:
+        copy.start()
+    for copy in tables:
+        copy.wait()
+
+    def cross_over(i):
+        held, landing = ((ra, both_a), (rb, both_b))[i]
+        drain(held, recv_a.at[i])
+        pltpu.make_async_copy(held, landing.at[pl.ds(0, 128)], recv_a.at[i]).start()
+        part = CROSS // CROSS_PARTS
+
+        for p in range(CROSS_PARTS):
+
+            def pack(k, carry):
+                xs[i, k] = held[cross[0, k]]
+                return carry
+
+            lax.fori_loop(p * part, p * part + part, pack, 0, unroll=2)
+            pltpu.make_async_remote_copy(
+                src_ref=xs.at[i, pl.ds(p * part, part)],
+                dst_ref=landing.at[pl.ds(128 + p * part, part)],
+                send_sem=send_b.at[i], recv_sem=recv_b.at[i],
+                device_id=(partner, head), device_id_type=MESH,
+            ).start()
+
+    def deliver(i, target, sem):
+        held, came = ((ra, both_a), (rb, both_b))[i]
+        drain(held, recv_a.at[i])
+        drain(xs.at[i], recv_b.at[i])
+
+        def pick(j):
+            group = group_at(j, half)
+            for a in range(4):
+                s2[i, j, a] = came[code[a, group]]
+
+        def send(k, carry):
+            j = jnp.bitwise_xor(plane, k)
+            pick(j)
+            pltpu.make_async_remote_copy(
+                src_ref=s2.at[i, j], dst_ref=target, send_sem=send_c.at[i], recv_sem=sem,
+                device_id=(group_at(j, half), head), device_id_type=MESH,
+            ).start()
+            return carry
+
+        lax.fori_loop(1, 32, send, 0)
+        pick(plane)
+        pltpu.make_async_copy(s2.at[i, plane], target, sem).start()
+
+    def share_out(attended, share, got, which):
+        def block(d, carry):
+            to = lax.rem(head + d, 4)
+            start = pl.multiple_of(to * 1024, 1024)
+            low = jnp.dot(attended, w[:, pl.ds(start, 512)], preferred_element_type=F32)
+            high = jnp.dot(attended, w[:, pl.ds(start + 512, 512)], preferred_element_type=F32)
+            share[to] = jnp.concatenate([low, high], axis=0).astype(BF16)
+
+            @pl.when(d < 4)
+            def _():
+                pltpu.make_async_remote_copy(
+                    src_ref=share.at[to], dst_ref=got.at[d - 1], send_sem=share_send.at[which],
+                    recv_sem=share_recv.at[which], device_id=(me, to), device_id_type=MESH,
+                ).start()
+
+            return carry
+
+        lax.fori_loop(1, 5, block, 0)
+
+    def share_in(share, got, which, out):
+        drain(got, share_recv.at[which])
+        total = share[head].astype(F32)
+        for d in range(3):
+            total = total + got[d].astype(F32)
+        out[...] = jnp.concatenate([total[0:8], total[8:16]], axis=1).astype(BF16)
+        drain(got, share_send.at[which])
+
+    @pl.when(is_relay0)
+    def _():
+        cross_over(0)
+
+    spread_tokens(2)
+    spread_tokens(3)
+    attended1 = attend(kv, reduce_query(q1[...], basis[...]), p1)
+    loads[10].wait()
+    share_out(attended1, share1, got1, 0)
+
+    @pl.when(jnp.logical_and(is_relay1, core == 0))
+    def _():
+        cross_over(1)
+
+    cols[...] = spread_columns(sf[...])
+    reduced2 = reduce_query(q2[...], basis[...])
+    tile0 = jnp.where(is_fresh, 36, 12 * core + my_q)
+
+    @pl.when(is_relay0)
+    def _():
+        deliver(0, r2.at[tile0], recv_c.at[0])
+
+    @pl.when(jnp.logical_and(is_relay1, core == 1))
+    def _():
+        cross_over(1)
+
+    share_in(share1, got1, 0, out1)
+    stores.append(pltpu.make_async_copy(out1, out1_hbm, local_sem.at[15]))
+    stores[-1].start()
+
+    @pl.when(jnp.logical_and(is_relay1, core == 0))
+    def _():
+        deliver(1, r2.at[24 + my_q], recv_c.at[0])
+
+    @pl.when(jnp.logical_and(is_relay1, core == 1))
+    def _():
+        deliver(1, r3.at[my_q], recv_c.at[1])
+
+    comes, keeps, p2 = [], [], []
+    drain(r2, recv_c.at[0])
+    news = []
+    lasts = []
+    for s in range(8):
+        come = jnp.int32(0)
+        stay = jnp.int32(1)
+        for a in range(4):
+            here = leave[a, me] == s
+            come = jnp.where(here, a, come)
+            stay = jnp.where(here, 0, stay)
+        origin = source[come, me]
+        group = origin // 4
+        last = jnp.where(stay == 1, p1[s], lens[leave[lax.rem(origin, 4), group], group])
+        kept = jnp.full((16, 128), stay, jnp.int32) == 1
+        comes.append(come)
+        keeps.append(kept)
+        lasts.append(last)
+        p2.append(last + 1)
+        new = jnp.where(kept, ft[s].astype(F32), r2[36, come].astype(F32))
+        news.append(jnp.concatenate([new[0:1], new[1:2, 0:64]], axis=1))
+    cols1[...] = spread_columns(jnp.concatenate(news, axis=0))
+
+    def settle(s, u, v):
+        a, b = 16 * u, 128 * v
+        tile = jnp.where(
+            keeps[s], kv[s, a : a + 16, b : b + 128].astype(F32), (r2[12 * v + u, comes[s]] if v < 3 else r3[u, comes[s]]).astype(F32)
+        )
+        fresh = cols[a : a + 16, 128 * s : 128 * s + 128].astype(F32)
+        fin[s, a : a + 16, b : b + 128] = jnp.where(lane + b == p2[s], fresh, tile).astype(BF16)
+
+    for s in range(8):
+        for u in range(12):
+            for v in range(3):
+                settle(s, u, v)
+            at = pl.ds(16 * u, 16)
+            wide_s = pl.ds(128 * s, 128)
+            tile = jnp.where(lane + 384 == lasts[s], cols1[at, wide_s].astype(F32), 0.0)
+            tile = jnp.where(lane + 384 == p2[s], cols[at, wide_s].astype(F32), tile)
+            fin[s, at, 384:512] = tile.astype(BF16)
+    stores.append(
+        pltpu.make_async_copy(
+            fin.at[:, :, pl.ds(0, 384)], cache_hbm.at[:, :, pl.ds(0, 384)], local_sem.at[16]
+        )
+    )
+    stores[-1].start()
+    share_out(attend(fin, reduced2, p2), share2, got2, 1)
+
+    drain(r3, recv_c.at[1])
+    for s in range(8):
+        for u in range(12):
+            settle(s, u, 3)
+    stores.append(
+        pltpu.make_async_copy(
+            fin.at[:, :, pl.ds(384, 128)], cache_hbm.at[:, :, pl.ds(384, 128)], local_sem.at[17]
+        )
+    )
+    stores[-1].start()
+    share_in(share2, got2, 1, out2)
+    stores.append(pltpu.make_async_copy(out2, out2_hbm, local_sem.at[18]))
+    stores[-1].start()
+
+    drain(s1.at[pl.ds(0, 47)], send_a.at[0])
+
+    @pl.when(turn == 0)
+    def _():
+        drain(s1.at[pl.ds(0, 1)], send_a.at[0])
+
+    @pl.when(jnp.logical_and(turn == 0, jnp.logical_not(is_fresh)))
+    def _():
+        drain(s1.at[pl.ds(0, 1)], send_a.at[0])
+
+    @pl.when(is_relay0)
+    def _():
+        drain(xs.at[0], send_b.at[0])
+        drain(s2.at[0, pl.ds(0, 31)], send_c.at[0])
+
+    @pl.when(is_relay1)
+    def _():
+        drain(xs.at[1], send_b.at[1])
+        drain(s2.at[1, pl.ds(0, 31)], send_c.at[1])
+
+    for store in stores:
+        store.wait()
+
+
 def hand_over(out1, out2, cache, to1, to2, to_cache, held, held1, held2, sem_in, sem_out):
     ways = [(cache.at[s], held.at[s], to_cache.at[s]) for s in range(8)]
     ways += [(out1, held1, to1), (out2, held2, to2)]
@@ -291,36 +653,45 @@
         copy.wait()
 
 
-def shards(
-    kv_cache, first_fresh, second_fresh, first_query, second_query, key_basis, out_weight,
-    lengths, leave_slot, arrive_row,
-):
-    kv = kv_cache[:, 0].transpose(0, 2, 1)
-    hbm = pl.BlockSpec(memory_space=pltpu.HBM)
-    out1, out2, cache = pl.pallas_call(
-        kernel,
-        out_shape=(
-            jax.ShapeDtypeStruct((8, 1024), BF16),
-            jax.ShapeDtypeStruct((8, 1024), BF16),
-            jax.ShapeDtypeStruct((8, 192, 512), BF16),
-        ),
-        in_specs=[hbm] * 10,
-        out_specs=(hbm, hbm, hbm),
-        scratch_shapes=[
-            pltpu.VMEM((8, 1024), BF16),
-            pltpu.VMEM((8, 1024), BF16),
-            pltpu.VMEM((8, 192, 512), BF16),
-            pltpu.SMEM((4, 64), jnp.int32),
-            pltpu.SMEM((4, 64), jnp.int32),
-            pltpu.SMEM((8, 64), jnp.int32),
-            pltpu.VMEM((4, 64), jnp.int32),
-            pltpu.VMEM((8, 192), BF16),
-            pltpu.VMEM((8, 192), BF16),
-            pltpu.VMEM((8, 1024), BF16),
-            pltpu.VMEM((8, 1024), BF16),
-            pltpu.VMEM((64, 128), BF16),
-            pltpu.VMEM((8, 192, 512), BF16),
-            pltpu.VMEM((1024, 4096), BF16),
+RESULTS = (
+    jax.ShapeDtypeStruct((8, 1024), BF16),
+    jax.ShapeDtypeStruct((8, 1024), BF16),
+    jax.ShapeDtypeStruct((8, 192, 512), BF16),
+)
+COMMON = [
+    pltpu.VMEM((8, 1024), BF16),
+    pltpu.VMEM((8, 1024), BF16),
+    pltpu.VMEM((8, 192, 512), BF16),
+    pltpu.SMEM((4, 64), jnp.int32),
+    pltpu.SMEM((4, 64), jnp.int32),
+    pltpu.SMEM((8, 64), jnp.int32),
+    pltpu.VMEM((4, 64), jnp.int32),
+    pltpu.VMEM((8, 192), BF16),
+    pltpu.VMEM((8, 192), BF16),
+    pltpu.VMEM((8, 1024), BF16),
+    pltpu.VMEM((8, 1024), BF16),
+    pltpu.VMEM((64, 128), BF16),
+    pltpu.VMEM((8, 192, 512), BF16),
+    pltpu.VMEM((1024, 4096), BF16),
+]
+SHARES = [
+    pltpu.VMEM((4, 16, 512), BF16),
+    pltpu.VMEM((4, 16, 512), BF16),
+    pltpu.VMEM((3, 16, 512), BF16),
+    pltpu.VMEM((3, 16, 512), BF16),
+]
+PAIR = pltpu.SemaphoreType.DMA((2,))
+HBM = pl.BlockSpec(memory_space=pltpu.HBM)
+
+
+def run_general(*operands):
+    return pl.pallas_call(
+        general_kernel,
+        out_shape=RESULTS,
+        in_specs=[HBM] * 10,
+        out_specs=[HBM] * 3,
+        scratch_shapes=COMMON
+        + [
             pltpu.VMEM((TILES, 4, 16, 128), BF16),
             pltpu.VMEM((64, 4, 16, 128), BF16),
             pltpu.VMEM((64, 4, 16, 128), BF16),
@@ -328,36 +699,83 @@
             pltpu.VMEM((4, 64), jnp.int32),
             pltpu.SMEM((4, 64), jnp.int32),
             pltpu.VMEM((192, 1024), BF16),
-            pltpu.VMEM((4, 16, 512), BF16),
-            pltpu.VMEM((4, 16, 512), BF16),
-            pltpu.VMEM((3, 16, 512), BF16),
-            pltpu.VMEM((3, 16, 512), BF16),
-            pltpu.SemaphoreType.DMA((15,)),
-            pltpu.SemaphoreType.DMA((2,)),
-            pltpu.SemaphoreType.DMA((2,)),
-            pltpu.SemaphoreType.DMA((2,)),
-            pltpu.SemaphoreType.DMA((2,)),
-        ],
+        ]
+        + SHARES
+        + [pltpu.SemaphoreType.DMA((15,)), PAIR, PAIR, PAIR, PAIR],
+        compiler_params=pltpu.CompilerParams(
+            collective_id=1, has_side_effects=True, vmem_limit_bytes=60 * 1024 * 1024
+        ),
+    )(*operands)
+
+
+def run_fast(*operands):
+    return pl.pallas_call(
+        fast_kernel,
+        out_shape=RESULTS + (jax.ShapeDtypeStruct((1, 1), jnp.int32),),
+        in_specs=[HBM] * 10,
+        out_specs=[HBM] * 3 + [pl.BlockSpec(memory_space=pltpu.SMEM)],
+        scratch_shapes=COMMON
+        + [
+            pltpu.VMEM((8, 16, 128), BF16),
+            pltpu.VMEM((49, 4, 16, 128), BF16),
+            pltpu.VMEM((128, 16, 128), BF16),
+            pltpu.VMEM((128, 16, 128), BF16),
+            pltpu.VMEM((2, CROSS, 16, 128), BF16),
+            pltpu.VMEM((128 + CROSS, 16, 128), BF16),
+            pltpu.VMEM((128 + CROSS, 16, 128), BF16),
+            pltpu.VMEM((2, 32, 4, 16, 128), BF16),
+            pltpu.VMEM((37, 4, 16, 128), BF16),
+            pltpu.VMEM((12, 4, 16, 128), BF16),
+            pltpu.VMEM((4, 64), jnp.int32),
+            pltpu.VMEM((4, 64), jnp.int32),
+            pltpu.VMEM((8, 128), jnp.int32),
+            pltpu.SMEM((4, 64), jnp.int32),
+            pltpu.SMEM((4, 64), jnp.int32),
+            pltpu.SMEM((8, 128), jnp.int32),
+            pltpu.VMEM((192, 1024), BF16),
+            pltpu.VMEM((192, 1024), BF16),
+        ]
+        + SHARES
+        + [pltpu.SemaphoreType.DMA((19,))]
+        + [PAIR] * 8,
         compiler_params=pltpu.CompilerParams(
             collective_id=0, has_side_effects=True, vmem_limit_bytes=60 * 1024 * 1024
         ),
-    )(
-        leave_slot.T, arrive_row.T, lengths.T, kv,
+    )(*operands)
+
+
+def pass_on(*results):
+    return pl.pallas_call(
+        hand_over,
+        out_shape=RESULTS,
+        in_specs=[HBM] * 3,
+        out_specs=[HBM] * 3,
+        scratch_shapes=[
+            pltpu.VMEM((8, 192, 512), BF16),
+            pltpu.VMEM((8, 1024), BF16),
+            pltpu.VMEM((8, 1024), BF16),
+            pltpu.SemaphoreType.DMA((10,)),
+            pltpu.SemaphoreType.DMA((10,)),
+        ],
+        compiler_params=pltpu.CompilerParams(vmem_limit_bytes=60 * 1024 * 1024),
+    )(*results)
+
+
+def shards(
+    kv_cache, first_fresh, second_fresh, first_query, second_query, key_basis, out_weight,
+    lengths, leave_slot, arrive_row,
+):
+    operands = (
+        leave_slot.T, arrive_row.T, lengths.T, kv_cache[:, 0].transpose(0, 2, 1),
         first_fresh[:, 0], second_fresh[:, 0], first_query[:, 0], second_query[:, 0],
         key_basis[0], out_weight,
     )
-    out1, out2, cache = pl.pallas_call(
-        hand_over,
-        out_shape=(
-            jax.ShapeDtypeStruct((8, 1024), BF16),
-            jax.ShapeDtypeStruct((8, 1024), BF16),
-            jax.ShapeDtypeStruct((8, 192, 512), BF16),
-        ),
-        in_specs=[hbm] * 3,
-        out_specs=(hbm, hbm, hbm),
-        scratch_shapes=[pltpu.VMEM((8, 192, 512), BF16), pltpu.VMEM((8, 1024), BF16), pltpu.VMEM((8, 1024), BF16), pltpu.SemaphoreType.DMA((10,)), pltpu.SemaphoreType.DMA((10,))],
-        compiler_params=pltpu.CompilerParams(vmem_limit_bytes=60 * 1024 * 1024),
-    )(out1, out2, cache)
+    *results, fits = run_fast(*operands)
+    out1, out2, cache = lax.cond(
+        fits[0, 0] == 1,
+        lambda: tuple(pass_on(*results)),
+        lambda: tuple(pass_on(*run_general(*operands))),
+    )
     return out1, out2, cache.transpose(0, 2, 1)[:, None]
 
 

time: 64.9 us -> 62.2 us (0.958); the launches traced: 64.1 us -> 62.1 us
  Pallas kernels: 63.5 us -> 60.6 us
  between operations: 0.64 us -> 1.41 us
    pallas_call x2, Pallas kernels: 63.5 us -> 60.6 us  [the longest x1 57.3 us: run_fast(): pl.pallas_call(fast_kernel, out_shape=RESULTS + (jax.ShapeDtypeStruct((1,...]
where the time goes in v3:
time: 62.2 us; the launch traced here: 62.1 us
  Pallas kernels  60.6 us (97%)
  between operations  1.41 us (2%)
    pallas_call x1, Pallas kernels, run_fast(): pl.pallas_call(fast_kernel, out_shape=RESULTS + (jax.ShapeDtypeStruct((1,...  57.3 us
    pallas_call x1, Pallas kernels, pass_on(): pl.pallas_call(hand_over, out_shape=RESULTS, in_specs=[HBM] * 3, out_spec...  3.38 us

profile of v3, /device:TPU:24, one launch (start us, length us, event | category | flops | bytes accessed | tf_op | source)
XLA Modules:
  0.0 62.1 jit_solution(10124088502799807966)
XLA Ops:
  0.6 0.0 copy-start
  0.6 0.0 copy-start.1
  0.7 0.0 copy-start.2
  0.7 0.0 copy-start.3
  0.7 0.0 copy-start.4
  0.7 0.0 copy-start.5
  0.7 0.0 copy-start.6
  0.7 0.0 copy-start.7
  0.7 0.0 copy-start.8
  0.7 57.3 %shard_map.121 = (bf16[8,1024]{1,0:T(8,128)(2,1)S(1)}, bf16[8,1024]{1,0:T(8,128)(2,1)S(1)}, bf16[8,192,512]{2,1,0:T(8,128)(2,1)S(1)}, s32[1,1]{1,0:T(1,128)}) custom-call(s32[4,64]{1,0:T(4,128)} %bitcast.29, s32[4,64]{1,0:T(4,128)} %bitcast.31, s32[8,64]{1,0:T(8,128)} %bitcast.23, bf16[8,192,512]{2,1,0:T(8,128)(2,1)} %bitcast.15, bf16[8,192]{1,0:T(8,128)(2,1)} %bitcast.25, ...), custom_call_target="tpu_custom_call" | custom-call | tf_op jit(solution)/shard_map/pallas_call | solution.py:712
  58.6 0.0 copy-done
  58.6 0.0 copy-done.1
  58.6 0.0 copy-done.2
  58.6 0.0 copy-done.3
  58.7 0.0 copy-done.4
  58.7 0.0 copy-done.5
  58.7 0.0 copy-done.6
  58.7 0.0 copy-done.7
  58.7 0.0 copy-done.8
  58.7 3.4 %conditional.1 = ((bf16[8,1024]{1,0:T(8,128)(2,1)}, bf16[8,1024]{1,0:T(8,128)(2,1)}, bf16[8,192,512]{2,1,0:T(8,128)(2,1)})) conditional(s32[]{:T(128)} %bitcast.10, (s32[4,64]{1,0:T(4,128)S(1)}, s32[4,64]{1,0:T(4,128)S(1)}, s32[8,64]{1,0:T(8,128)S(1)}, bf16[8,192,512]{2,1,0:T(8,128)(2,1)S(1)}, bf16[8,192]{1,0:T(8,128)(2,1)S(1)}, ...), branch_computations={%region_0.0_spmd, %region_1.0_spmd} | conditional | bytes 8 | solution.py:774
  58.7 3.4 %branch_1_fun.1 = (bf16[8,1024]{1,0:T(8,128)(2,1)}, bf16[8,1024]{1,0:T(8,128)(2,1)}, bf16[8,192,512]{2,1,0:T(8,128)(2,1)}) custom-call(bf16[8,1024]{1,0:T(8,128)(2,1)S(1)} %get-tuple-element.39.out1, bf16[8,1024]{1,0:T(8,128)(2,1)S(1)} %get-tuple-element.40.out2, bf16[8,192,512]{2,1,0:T(8,128)(2,1)S(1)} %get-tuple-element.41.cache), custom_call_target="tpu_custom_call" | custom-call | tf_op jit(solution)/shard_map/cond/branch_1_fun/pallas_call | solution.py:748
Async XLA Ops:
  0.6 58.0 %copy-start = (bf16[8,1,512,192]{2,3,1,0:T(8,128)(2,1)S(1)}, bf16[8,1,512,192]{2,3,1,0:T(8,128)(2,1)}, u32[]{:S(2)}) copy-start(bf16[8,1,512,192]{2,3,1,0:T(8,128)(2,1)} %param.12) | copy-start | bytes 4718596
  0.6 58.0 %copy-start.1 = (bf16[8,1,1024]{2,0,1:T(8,128)(2,1)S(1)}, bf16[8,1,1024]{2,0,1:T(8,128)(2,1)}, u32[]{:S(2)}) copy-start(bf16[8,1,1024]{2,0,1:T(8,128)(2,1)} %param.15) | copy-start | bytes 49156
  0.7 58.0 %copy-start.2 = (bf16[8,1,1024]{2,0,1:T(8,128)(2,1)S(1)}, bf16[8,1,1024]{2,0,1:T(8,128)(2,1)}, u32[]{:S(2)}) copy-start(bf16[8,1,1024]{2,0,1:T(8,128)(2,1)} %param.16) | copy-start | bytes 49156
  0.7 58.0 %copy-start.3 = (bf16[1,64,128]{2,1,0:T(8,128)(2,1)S(1)}, bf16[1,64,128]{2,1,0:T(8,128)(2,1)}, u32[]{:S(2)}) copy-start(bf16[1,64,128]{2,1,0:T(8,128)(2,1)} %param.17) | copy-start | bytes 49156
  0.7 58.0 %copy-start.4 = (s32[64,8]{0,1:T(8,128)S(1)}, s32[64,8]{0,1:T(8,128)}, u32[]{:S(2)}) copy-start(s32[64,8]{0,1:T(8,128)} %param.19) | copy-start | bytes 6148
  0.7 58.0 %copy-start.5 = (bf16[8,1,192]{2,0,1:T(8,128)(2,1)S(1)}, bf16[8,1,192]{2,0,1:T(8,128)(2,1)}, u32[]{:S(2)}) copy-start(bf16[8,1,192]{2,0,1:T(8,128)(2,1)} %param.13) | copy-start | bytes 9220
  0.7 58.0 %copy-start.6 = (bf16[8,1,192]{2,0,1:T(8,128)(2,1)S(1)}, bf16[8,1,192]{2,0,1:T(8,128)(2,1)}, u32[]{:S(2)}) copy-start(bf16[8,1,192]{2,0,1:T(8,128)(2,1)} %param.14) | copy-start | bytes 9220
  0.7 58.0 %copy-start.7 = (s32[64,4]{0,1:T(4,128)S(1)}, s32[64,4]{0,1:T(4,128)}, u32[]{:S(2)}) copy-start(s32[64,4]{0,1:T(4,128)} %param.20) | copy-start | bytes 3076
  0.7 58.0 %copy-start.8 = (s32[64,4]{0,1:T(4,128)S(1)}, s32[64,4]{0,1:T(4,128)}, u32[]{:S(2)}) copy-start(s32[64,4]{0,1:T(4,128)} %param.21) | copy-start | bytes 3076

commit v4 on v3

--- a/solution.py
+++ b/solution.py
@@ -744,6 +744,29 @@
     )(*operands)
 
 
+def hand_straight(out1, out2, cache, to1, to2, to_cache, sem):
+    copies = [
+        pltpu.make_async_copy(cache.at[s], to_cache.at[s], sem.at[s]) for s in range(8)
+    ]
+    copies.append(pltpu.make_async_copy(out1, to1, sem.at[8]))
+    copies.append(pltpu.make_async_copy(out2, to2, sem.at[9]))
+    for copy in copies:
+        copy.start()
+    for copy in copies:
+        copy.wait()
+
+
+def pass_straight(*results):
+    return pl.pallas_call(
+        hand_straight,
+        out_shape=RESULTS,
+        in_specs=[pl.BlockSpec(memory_space=pltpu.VMEM)] * 3,
+        out_specs=[HBM] * 3,
+        scratch_shapes=[pltpu.SemaphoreType.DMA((10,))],
+        compiler_params=pltpu.CompilerParams(vmem_limit_bytes=16 * 1024 * 1024),
+    )(*results)
+
+
 def pass_on(*results):
     return pl.pallas_call(
         hand_over,
@@ -773,7 +796,7 @@
     *results, fits = run_fast(*operands)
     out1, out2, cache = lax.cond(
         fits[0, 0] == 1,
-        lambda: tuple(pass_on(*results)),
+        lambda: tuple(pass_straight(*results)),
         lambda: tuple(pass_on(*run_general(*operands))),
     )
     return out1, out2, cache.transpose(0, 2, 1)[:, None]

time: 62.2 us -> 60 us (0.965)
  Pallas kernels: 60.6 us -> 58.5 us
    pallas_call x1, Pallas kernels: 3.38 us -> 1.22 us  [pass_straight(): pl.pallas_call(hand_straight, out_shape=RESULTS, in_specs=[pl.BlockSpec(m...]
where the time goes in v4:
time: 60 us; the launch traced here: 59.9 us
  Pallas kernels  58.5 us (98%)
  between operations  1.41 us (2%)
    pallas_call x1, Pallas kernels, run_fast(): pl.pallas_call(fast_kernel, out_shape=RESULTS + (jax.ShapeDtypeStruct((1,...  57.3 us
    pallas_call x1, Pallas kernels, pass_straight(): pl.pallas_call(hand_straight, out_shape=RESULTS, in_specs=[pl.BlockSpec(m...  1.22 us

profile of v4, /device:TPU:24, one launch (start us, length us, event | category | flops | bytes accessed | tf_op | source)
XLA Modules:
  0.0 59.9 jit_solution(18243986445045856049)
XLA Ops:
  0.6 0.0 copy-start
  0.6 0.0 copy-start.1
  0.7 0.0 copy-start.2
  0.7 0.0 copy-start.3
  0.7 0.0 copy-start.4
  0.7 0.0 copy-start.5
  0.7 0.0 copy-start.6
  0.7 0.0 copy-start.7
  0.7 0.0 copy-start.8
  0.7 57.3 %shard_map.121 = (bf16[8,1024]{1,0:T(8,128)(2,1)S(1)}, bf16[8,1024]{1,0:T(8,128)(2,1)S(1)}, bf16[8,192,512]{2,1,0:T(8,128)(2,1)S(1)}, s32[1,1]{1,0:T(1,128)}) custom-call(s32[4,64]{1,0:T(4,128)} %bitcast.29, s32[4,64]{1,0:T(4,128)} %bitcast.31, s32[8,64]{1,0:T(8,128)} %bitcast.23, bf16[8,192,512]{2,1,0:T(8,128)(2,1)} %bitcast.15, bf16[8,192]{1,0:T(8,128)(2,1)} %bitcast.25, ...), custom_call_target="tpu_custom_call" | custom-call | tf_op jit(solution)/shard_map/pallas_call | solution.py:712
  58.6 0.0 copy-done
  58.6 0.0 copy-done.1
  58.6 0.0 copy-done.2
  58.6 0.0 copy-done.3
  58.7 0.0 copy-done.4
  58.7 0.0 copy-done.5
  58.7 0.0 copy-done.6
  58.7 0.0 copy-done.7
  58.7 0.0 copy-done.8
  58.7 1.2 %conditional.1 = ((bf16[8,1024]{1,0:T(8,128)(2,1)}, bf16[8,1024]{1,0:T(8,128)(2,1)}, bf16[8,192,512]{2,1,0:T(8,128)(2,1)})) conditional(s32[]{:T(128)} %bitcast.10, (s32[4,64]{1,0:T(4,128)S(1)}, s32[4,64]{1,0:T(4,128)S(1)}, s32[8,64]{1,0:T(8,128)S(1)}, bf16[8,192,512]{2,1,0:T(8,128)(2,1)S(1)}, bf16[8,192]{1,0:T(8,128)(2,1)S(1)}, ...), branch_computations={%region_0.0_spmd, %region_1.0_spmd} | conditional | bytes 8 | solution.py:797
  58.7 1.2 %branch_1_fun.1 = (bf16[8,1024]{1,0:T(8,128)(2,1)}, bf16[8,1024]{1,0:T(8,128)(2,1)}, bf16[8,192,512]{2,1,0:T(8,128)(2,1)}) custom-call(bf16[8,1024]{1,0:T(8,128)(2,1)S(1)} %get-tuple-element.39.out1, bf16[8,1024]{1,0:T(8,128)(2,1)S(1)} %get-tuple-element.40.out2, bf16[8,192,512]{2,1,0:T(8,128)(2,1)S(1)} %get-tuple-element.41.cache), custom_call_target="tpu_custom_call" | custom-call | tf_op jit(solution)/shard_map/cond/branch_1_fun/pallas_call | solution.py:760
Async XLA Ops:
  0.6 58.0 %copy-start = (bf16[8,1,512,192]{2,3,1,0:T(8,128)(2,1)S(1)}, bf16[8,1,512,192]{2,3,1,0:T(8,128)(2,1)}, u32[]{:S(2)}) copy-start(bf16[8,1,512,192]{2,3,1,0:T(8,128)(2,1)} %param.12) | copy-start | bytes 4718596
  0.6 58.0 %copy-start.1 = (bf16[8,1,1024]{2,0,1:T(8,128)(2,1)S(1)}, bf16[8,1,1024]{2,0,1:T(8,128)(2,1)}, u32[]{:S(2)}) copy-start(bf16[8,1,1024]{2,0,1:T(8,128)(2,1)} %param.15) | copy-start | bytes 49156
  0.7 58.0 %copy-start.2 = (bf16[8,1,1024]{2,0,1:T(8,128)(2,1)S(1)}, bf16[8,1,1024]{2,0,1:T(8,128)(2,1)}, u32[]{:S(2)}) copy-start(bf16[8,1,1024]{2,0,1:T(8,128)(2,1)} %param.16) | copy-start | bytes 49156
  0.7 58.0 %copy-start.3 = (bf16[1,64,128]{2,1,0:T(8,128)(2,1)S(1)}, bf16[1,64,128]{2,1,0:T(8,128)(2,1)}, u32[]{:S(2)}) copy-start(bf16[1,64,128]{2,1,0:T(8,128)(2,1)} %param.17) | copy-start | bytes 49156
  0.7 58.0 %copy-start.4 = (s32[64,8]{0,1:T(8,128)S(1)}, s32[64,8]{0,1:T(8,128)}, u32[]{:S(2)}) copy-start(s32[64,8]{0,1:T(8,128)} %param.19) | copy-start | bytes 6148
  0.7 58.0 %copy-start.5 = (bf16[8,1,192]{2,0,1:T(8,128)(2,1)S(1)}, bf16[8,1,192]{2,0,1:T(8,128)(2,1)}, u32[]{:S(2)}) copy-start(bf16[8,1,192]{2,0,1:T(8,128)(2,1)} %param.13) | copy-start | bytes 9220
  0.7 58.0 %copy-start.6 = (bf16[8,1,192]{2,0,1:T(8,128)(2,1)S(1)}, bf16[8,1,192]{2,0,1:T(8,128)(2,1)}, u32[]{:S(2)}) copy-start(bf16[8,1,192]{2,0,1:T(8,128)(2,1)} %param.14) | copy-start | bytes 9220
  0.7 58.0 %copy-start.7 = (s32[64,4]{0,1:T(4,128)S(1)}, s32[64,4]{0,1:T(4,128)}, u32[]{:S(2)}) copy-start(s32[64,4]{0,1:T(4,128)} %param.20) | copy-start | bytes 3076
  0.7 58.0 %copy-start.8 = (s32[64,4]{0,1:T(4,128)S(1)}, s32[64,4]{0,1:T(4,128)}, u32[]{:S(2)}) copy-start(s32[64,4]{0,1:T(4,128)} %param.21) | copy-start | bytes 3076

commit v5 on v4

--- a/solution.py
+++ b/solution.py
@@ -376,7 +376,7 @@
             for u in range(12):
                 at = (s, pl.ds(16 * u, 16), pl.ds(128 * v, 128))
                 fresh = cols[pl.ds(16 * u, 16), pl.ds(128 * s, 128)]
-                kv[at] = jnp.where(hit, fresh.astype(F32), kv[at].astype(F32)).astype(BF16)
+                kv[at] = jnp.where(hit, fresh, kv[at])
 
     rows = [leave[m, me] for m in range(4)]
     for m in range(4):
@@ -404,6 +404,7 @@
 
     spread_tokens(0)
     spread_tokens(1)
+    spread_tokens(2)
     for load in loads[4:10]:
         load.wait()
 
@@ -519,7 +520,6 @@
     def _():
         cross_over(0)
 
-    spread_tokens(2)
     spread_tokens(3)
     attended1 = attend(kv, reduce_query(q1[...], basis[...]), p1)
     loads[10].wait()
@@ -578,11 +578,10 @@
 
     def settle(s, u, v):
         a, b = 16 * u, 128 * v
-        tile = jnp.where(
-            keeps[s], kv[s, a : a + 16, b : b + 128].astype(F32), (r2[12 * v + u, comes[s]] if v < 3 else r3[u, comes[s]]).astype(F32)
-        )
-        fresh = cols[a : a + 16, 128 * s : 128 * s + 128].astype(F32)
-        fin[s, a : a + 16, b : b + 128] = jnp.where(lane + b == p2[s], fresh, tile).astype(BF16)
+        came = r2[12 * v + u, comes[s]] if v < 3 else r3[u, comes[s]]
+        tile = jnp.where(keeps[s], kv[s, a : a + 16, b : b + 128], came)
+        fresh = cols[a : a + 16, 128 * s : 128 * s + 128]
+        fin[s, a : a + 16, b : b + 128] = jnp.where(lane + b == p2[s], fresh, tile)
 
     for s in range(8):
         for u in range(12):

time: 60 us -> 59.5 us (level)
  Pallas kernels: 58.5 us -> 57.9 us
where the time goes in v5:
time: 59.5 us; the launch traced here: 59.4 us
  Pallas kernels  57.9 us (97%)
  between operations  1.41 us (2%)
    pallas_call x1, Pallas kernels, run_fast(): pl.pallas_call(fast_kernel, out_shape=RESULTS + (jax.ShapeDtypeStruct((1,...  56.7 us
    pallas_call x1, Pallas kernels, pass_straight(): pl.pallas_call(hand_straight, out_shape=RESULTS, in_specs=[pl.BlockSpec(m...  1.22 us

profile of v5, /device:TPU:24, one launch (start us, length us, event | category | flops | bytes accessed | tf_op | source)
XLA Modules:
  0.0 59.4 jit_solution(9737828780848573053)
XLA Ops:
  0.6 0.0 copy-start
  0.6 0.0 copy-start.1
  0.7 0.0 copy-start.2
  0.7 0.0 copy-start.3
  0.7 0.0 copy-start.4
  0.7 0.0 copy-start.5
  0.7 0.0 copy-start.6
  0.7 0.0 copy-start.7
  0.7 0.0 copy-start.8
  0.7 56.7 %shard_map.121 = (bf16[8,1024]{1,0:T(8,128)(2,1)S(1)}, bf16[8,1024]{1,0:T(8,128)(2,1)S(1)}, bf16[8,192,512]{2,1,0:T(8,128)(2,1)S(1)}, s32[1,1]{1,0:T(1,128)}) custom-call(s32[4,64]{1,0:T(4,128)} %bitcast.29, s32[4,64]{1,0:T(4,128)} %bitcast.31, s32[8,64]{1,0:T(8,128)} %bitcast.23, bf16[8,192,512]{2,1,0:T(8,128)(2,1)} %bitcast.15, bf16[8,192]{1,0:T(8,128)(2,1)} %bitcast.25, ...), custom_call_target="tpu_custom_call" | custom-call | tf_op jit(solution)/shard_map/pallas_call | solution.py:711
  58.1 0.0 copy-done
  58.1 0.0 copy-done.1
  58.1 0.0 copy-done.2
  58.1 0.0 copy-done.3
  58.1 0.0 copy-done.4
  58.1 0.0 copy-done.5
  58.1 0.0 copy-done.6
  58.1 0.0 copy-done.7
  58.2 0.0 copy-done.8
  58.2 1.2 %conditional.1 = ((bf16[8,1024]{1,0:T(8,128)(2,1)}, bf16[8,1024]{1,0:T(8,128)(2,1)}, bf16[8,192,512]{2,1,0:T(8,128)(2,1)})) conditional(s32[]{:T(128)} %bitcast.10, (s32[4,64]{1,0:T(4,128)S(1)}, s32[4,64]{1,0:T(4,128)S(1)}, s32[8,64]{1,0:T(8,128)S(1)}, bf16[8,192,512]{2,1,0:T(8,128)(2,1)S(1)}, bf16[8,192]{1,0:T(8,128)(2,1)S(1)}, ...), branch_computations={%region_0.0_spmd, %region_1.0_spmd} | conditional | bytes 8 | solution.py:796
  58.2 1.2 %branch_1_fun.1 = (bf16[8,1024]{1,0:T(8,128)(2,1)}, bf16[8,1024]{1,0:T(8,128)(2,1)}, bf16[8,192,512]{2,1,0:T(8,128)(2,1)}) custom-call(bf16[8,1024]{1,0:T(8,128)(2,1)S(1)} %get-tuple-element.39.out1, bf16[8,1024]{1,0:T(8,128)(2,1)S(1)} %get-tuple-element.40.out2, bf16[8,192,512]{2,1,0:T(8,128)(2,1)S(1)} %get-tuple-element.41.cache), custom_call_target="tpu_custom_call" | custom-call | tf_op jit(solution)/shard_map/cond/branch_1_fun/pallas_call | solution.py:759
Async XLA Ops:
  0.6 57.4 %copy-start = (bf16[8,1,512,192]{2,3,1,0:T(8,128)(2,1)S(1)}, bf16[8,1,512,192]{2,3,1,0:T(8,128)(2,1)}, u32[]{:S(2)}) copy-start(bf16[8,1,512,192]{2,3,1,0:T(8,128)(2,1)} %param.12) | copy-start | bytes 4718596
  0.6 57.4 %copy-start.1 = (bf16[8,1,1024]{2,0,1:T(8,128)(2,1)S(1)}, bf16[8,1,1024]{2,0,1:T(8,128)(2,1)}, u32[]{:S(2)}) copy-start(bf16[8,1,1024]{2,0,1:T(8,128)(2,1)} %param.15) | copy-start | bytes 49156
  0.7 57.4 %copy-start.2 = (bf16[8,1,1024]{2,0,1:T(8,128)(2,1)S(1)}, bf16[8,1,1024]{2,0,1:T(8,128)(2,1)}, u32[]{:S(2)}) copy-start(bf16[8,1,1024]{2,0,1:T(8,128)(2,1)} %param.16) | copy-start | bytes 49156
  0.7 57.4 %copy-start.3 = (bf16[1,64,128]{2,1,0:T(8,128)(2,1)S(1)}, bf16[1,64,128]{2,1,0:T(8,128)(2,1)}, u32[]{:S(2)}) copy-start(bf16[1,64,128]{2,1,0:T(8,128)(2,1)} %param.17) | copy-start | bytes 49156
  0.7 57.4 %copy-start.4 = (s32[64,8]{0,1:T(8,128)S(1)}, s32[64,8]{0,1:T(8,128)}, u32[]{:S(2)}) copy-start(s32[64,8]{0,1:T(8,128)} %param.19) | copy-start | bytes 6148
  0.7 57.4 %copy-start.5 = (bf16[8,1,192]{2,0,1:T(8,128)(2,1)S(1)}, bf16[8,1,192]{2,0,1:T(8,128)(2,1)}, u32[]{:S(2)}) copy-start(bf16[8,1,192]{2,0,1:T(8,128)(2,1)} %param.13) | copy-start | bytes 9220
  0.7 57.4 %copy-start.6 = (bf16[8,1,192]{2,0,1:T(8,128)(2,1)S(1)}, bf16[8,1,192]{2,0,1:T(8,128)(2,1)}, u32[]{:S(2)}) copy-start(bf16[8,1,192]{2,0,1:T(8,128)(2,1)} %param.14) | copy-start | bytes 9220
  0.7 57.4 %copy-start.7 = (s32[64,4]{0,1:T(4,128)S(1)}, s32[64,4]{0,1:T(4,128)}, u32[]{:S(2)}) copy-start(s32[64,4]{0,1:T(4,128)} %param.20) | copy-start | bytes 3076
  0.7 57.4 %copy-start.8 = (s32[64,4]{0,1:T(4,128)S(1)}, s32[64,4]{0,1:T(4,128)}, u32[]{:S(2)}) copy-start(s32[64,4]{0,1:T(4,128)} %param.21) | copy-start | bytes 3076
